TPU v7x, 32 devices: a whole 2x2x4 slice. The times are simulated.
32 devices in a mesh: sample: 4 (over y, core), tok: 8 (over z, x).
Axes of the slice: x: 2, y: 2, z: 4, core: 2. Of those that a mesh axis runs over, the one named last changes fastest.
Arguments:
- noisy_pos: float32 [4, 3, 4096], P('sample', None, 'tok'), may hold values from -384 to 384
- noise_step: int32 [1], replicated, may hold values from 60 to 120
- atom_single: bfloat16 [4096, 128], P('tok'), may hold values from -6 to 6
- atom_token: int32 [4096], P('tok'), may hold values from 0 to 511, as said below
- token_counts: int32 [512], P('tok'), may hold values from 1 to 29, as said below
- atom_bias: bfloat16 [4096, 2, 4, 128], P('tok'), may hold values from -400 to 400
- token_single: bfloat16 [512, 768], P('tok'), may hold values from -6 to 6
- pair_bias: bfloat16 [2, 16, 512, 512], P(None, 'sample', 'tok'), may hold values from -400 to 400
- w_pos: float32 [3, 128], replicated, may hold values from -3.5 to 3.5
- w_atom: bfloat16 [2, 128, 512], replicated, may hold values from -0.5 to 0.5
- w_atom_out: bfloat16 [2, 128, 128], replicated, may hold values from -0.5 to 0.5
- w_tok_in: bfloat16 [128, 768], replicated, may hold values from -0.5 to 0.5
- w_proj: bfloat16 [2, 3, 768, 768], replicated, may hold values from -0.21875 to 0.21875
- w_out: bfloat16 [2, 16, 48, 768], replicated, may hold values from -0.21875 to 0.21875
- w_tok_out: bfloat16 [768, 128], replicated, may hold values from -0.21875 to 0.21875
- w_pos_out: bfloat16 [3, 128], replicated, may hold values from -0.5 to 0.5
Outputs:
- denoised: float32 [4, 3, 4096], P('sample', None, 'tok')
Inputs may be any that keep to these rules, and one draw needn't show every extreme that they name: Atoms are ordered by token: atom_token never falls, token t owns exactly token_counts[t] consecutive atoms, and every token owns one atom or more. `token_counts`: they sum to 4096; each of the first 128 tokens has 23 to 29 atoms, each other token 1 to 3; token 0 has 29.
All inputs are finite; a program needn't handle non-finite values.
Results may differ from a plain program's by a relative error of at most 0.012.
Values may be sent and summed in bfloat16 or wider, within the bound.
A program may use at most 128 MiB of HBM per device.

v0:
```python
import math

import jax
import jax.numpy as jnp
from jax import lax
from jax.sharding import PartitionSpec as P

WQ = 32
WK = 128
RIM = 80


sigma_data = 16.0
sigma_peak = 160.0
sigma_floor = 0.0004
plan_steps = 200.0
norm_eps = 1e-05
masked_score = -1000000000.0
start_max = -1e30


def padded_2(block, sides, width):
    for axis, dim in sides:
        count = lax.axis_size(axis)
        forward = [(i, i + 1) for i in range(count - 1)]
        backward = [(target, source) for source, target in forward]
        low = lax.ppermute(
            lax.slice_in_dim(block, block.shape[dim] - width, None, axis=dim), axis, forward
        )
        high = lax.ppermute(lax.slice_in_dim(block, 0, width, axis=dim), axis, backward)
        block = jnp.concatenate([low, block, high], axis=dim)
    return block


def noise_level(noise_step):
    fraction = noise_step[0].astype(jnp.float32) / plan_steps
    upper = sigma_peak ** (1.0 / 7.0)
    lower = sigma_floor ** (1.0 / 7.0)
    return sigma_data * (upper + fraction * (lower - upper)) ** 7


def layer_norm(values):
    centred = values - jnp.mean(values, axis=-1, keepdims=True)
    spread = jnp.mean(centred * centred, axis=-1, keepdims=True)
    return centred / jnp.sqrt(spread + norm_eps)


def key_windows(padded, windows):
    blocks = padded.reshape(padded.shape[0], -1, WQ, padded.shape[-1])
    pieces = [blocks[:, 1 + offset : 1 + offset + windows] for offset in range(WK // WQ)]
    return jnp.concatenate(pieces, axis=2)


def atom_layer(atom_act, weights, out_weights, bias, first_atom, atom_total):
    samples, atom_count, width = atom_act.shape
    head_count = bias.shape[1]
    head_dim = width // head_count
    windows = atom_count // WQ
    normed = layer_norm(atom_act).astype(jnp.bfloat16)
    projected = jnp.dot(normed, weights, preferred_element_type=jnp.float32)
    query_rows = projected[..., :width].astype(jnp.bfloat16)
    gate_rows = projected[..., 3 * width :]
    paired = padded_2(projected[..., width : 3 * width].astype(jnp.bfloat16), (("tok", 1),), RIM)
    window_keys = key_windows(paired[..., :width], windows).reshape(
        samples, windows, WK, head_count, head_dim
    )
    window_values = key_windows(paired[..., width:], windows).reshape(
        samples, windows, WK, head_count, head_dim
    )
    window_queries = query_rows.reshape(samples, windows, WQ, head_count, head_dim)
    score_scale = 1.0 / math.sqrt(head_dim)
    scores = (
        jnp.einsum(
            "swqhd,swkhd->swhqk", window_queries, window_keys, preferred_element_type=jnp.float32
        )
        * score_scale
    )
    scores = (
        scores
        + bias.reshape(windows, WQ, head_count, WK).transpose(0, 2, 1, 3).astype(jnp.float32)[None]
    )
    positions = (
        first_atom + WQ * jnp.arange(windows)[:, None] - (WK - WQ) // 2 + jnp.arange(WK)[None, :]
    )
    valid = (positions >= 0) & (positions < atom_total)
    scores = jnp.where(valid[None, :, None, None, :], scores, masked_score)
    row_max = jnp.max(scores, axis=-1, keepdims=True)
    exponent = jnp.exp(scores - row_max)
    mixed = jnp.einsum(
        "swhqk,swkhd->swqhd",
        exponent.astype(jnp.bfloat16),
        window_values,
        preferred_element_type=jnp.float32,
    )
    mixed = mixed / jnp.transpose(jnp.sum(exponent, axis=-1, keepdims=True), (0, 1, 3, 2, 4))
    gated = (mixed.reshape(samples, atom_count, width) * jax.nn.sigmoid(gate_rows)).astype(
        jnp.bfloat16
    )
    return atom_act + jnp.dot(gated, out_weights, preferred_element_type=jnp.float32)


def attention_step(query_rows, bias, score_scale):

    def absorb(carry, pieces, start):
        row_max, row_sum, weighted = carry
        key_piece, value_piece = pieces
        bias_piece = bias.astype(jnp.float32)
        scores = (
            jnp.einsum("qshd,kshd->shqk", query_rows, key_piece, preferred_element_type=jnp.float32)
            * score_scale
            + bias_piece[None]
        )
        new_max = jnp.maximum(row_max, jnp.max(scores, axis=-1))
        exponent = jnp.exp(scores - new_max[..., None])
        row_sum = jnp.sum(exponent, axis=-1)
        weighted = jnp.einsum(
            "shqk,kshd->shqd",
            exponent.astype(jnp.bfloat16),
            value_piece,
            preferred_element_type=jnp.float32,
        )
        return (new_max, row_sum, weighted)

    return absorb


def initial_state(samples, head_count, token_count, head_dim):
    return (
        jnp.full((samples, head_count, token_count), start_max, jnp.float32),
        jnp.zeros((samples, head_count, token_count), jnp.float32),
        jnp.zeros((samples, head_count, token_count, head_dim), jnp.float32),
    )


def split_heads(projected, head_count, head_dim):
    token_count, samples = (projected.shape[1], projected.shape[2])
    shaped = projected.reshape(3, token_count, samples, head_count, head_dim)
    return (shaped[0], shaped[1], shaped[2])


def sample_block(token_act, proj, out_weights, bias):
    token_count, samples, model = token_act.shape
    head_count = out_weights.shape[0]
    head_dim = out_weights.shape[1]
    normed = layer_norm(token_act).astype(jnp.bfloat16)
    projected = jnp.einsum(
        "tsc,xcd->xtsd", normed, proj, preferred_element_type=jnp.float32
    ).astype(jnp.bfloat16)
    query_rows, key_rows, value_rows = split_heads(projected, head_count, head_dim)
    absorb = attention_step(query_rows, bias, 1.0 / math.sqrt(head_dim))
    start_state = initial_state(samples, head_count, token_count, head_dim)
    row_max, row_sum, weighted = absorb(
        start_state,
        (
            lax.all_gather(key_rows, "tok", axis=0, tiled=True),
            lax.all_gather(value_rows, "tok", axis=0, tiled=True),
        ),
        jnp.int32(0),
    )
    mixed = (weighted / row_sum[..., None]).astype(jnp.bfloat16)
    return token_act + jnp.einsum(
        "shqd,hdc->qsc", mixed, out_weights, preferred_element_type=jnp.float32
    )


def on_device(
    noisy_pos,
    noise_step,
    atom_single,
    atom_token,
    token_counts,
    atom_bias,
    token_single,
    pair_bias,
    w_pos,
    w_atom,
    w_atom_out,
    w_tok_in,
    w_proj,
    w_out,
    w_tok_out,
    w_pos_out,
):
    samples = noisy_pos.shape[0]
    atom_count = noisy_pos.shape[2]
    token_count = token_single.shape[0]
    width = atom_single.shape[1]
    first_atom = lax.axis_index("tok") * atom_count
    atom_total = atom_count * lax.axis_size("tok")
    sigma = noise_level(noise_step)
    square = sigma * sigma + sigma_data * sigma_data
    scale_in = 1.0 / jnp.sqrt(square)
    scale_skip = sigma_data * sigma_data / square
    scale_out = sigma * sigma_data / jnp.sqrt(square)
    placed = jnp.transpose(noisy_pos * scale_in, (0, 2, 1))
    atom_act = atom_single.astype(jnp.float32)[None] + jnp.dot(
        placed, w_pos, precision=lax.Precision.HIGHEST
    )
    for layer in range(w_atom.shape[0]):
        atom_act = atom_layer(
            atom_act, w_atom[layer], w_atom_out[layer], atom_bias[:, layer], first_atom, atom_total
        )
    lifted = jax.nn.relu(atom_act).astype(jnp.bfloat16)
    atom_rows = jnp.transpose(lifted, (1, 0, 2)).reshape(atom_count, samples * width)
    owners = jnp.arange(token_count * lax.axis_size("tok"))[:, None]
    onehot = (atom_token[None, :] == owners).astype(jnp.bfloat16)
    pooled = lax.psum_scatter(
        jnp.dot(onehot, atom_rows, preferred_element_type=jnp.float32).astype(jnp.bfloat16),
        "tok",
        scatter_dimension=0,
        tiled=True,
    ).astype(jnp.float32)
    token_mean = (
        pooled.reshape(token_count, samples, width)
        / token_counts[:, None, None].astype(jnp.float32)
    ).astype(jnp.bfloat16)
    token_act = token_single.astype(jnp.float32)[:, None, :] + jnp.dot(
        token_mean, w_tok_in, preferred_element_type=jnp.float32
    )
    bias_all = lax.all_gather(pair_bias, "sample", axis=1, tiled=True)
    for block in range(w_proj.shape[0]):
        token_act = sample_block(token_act, w_proj[block], w_out[block], bias_all[block])
    token_emit = jnp.dot(
        layer_norm(token_act).astype(jnp.bfloat16), w_tok_out, preferred_element_type=jnp.float32
    ).astype(jnp.bfloat16)
    emit_rows = token_emit.reshape(token_count, samples * width)

    def spread(carried, piece, start):
        owners = jnp.arange(piece.shape[0])[None, :]
        onehot = (atom_token[:, None] == owners).astype(jnp.bfloat16)
        return jnp.dot(onehot, piece, preferred_element_type=jnp.float32)

    empty = jnp.zeros((atom_count, samples * width), jnp.float32)
    received = spread(empty, lax.all_gather(emit_rows, "tok", axis=0, tiled=True), jnp.int32(0))
    atom_final = atom_act + jnp.transpose(received.reshape(atom_count, samples, width), (1, 0, 2))
    atom_out = layer_norm(atom_final).astype(jnp.bfloat16)
    update = jnp.einsum("xc,sac->sxa", w_pos_out, atom_out, preferred_element_type=jnp.float32)
    return (scale_skip * noisy_pos + scale_out * update) / sigma_data


def solution(mesh):
    in_specs = (
        P("sample", None, "tok"),
        P(),
        P("tok", None),
        P("tok"),
        P("tok"),
        P("tok", None, None, None),
        P("tok", None),
        P(None, "sample", "tok", None),
        P(),
        P(),
        P(),
        P(),
        P(),
        P(),
        P(),
        P(),
    )
    out_specs = P("sample", None, "tok")
    return jax.shard_map(
        on_device, mesh=mesh, in_specs=in_specs, out_specs=out_specs, check_vma=False
    )
```

profile of v0, /device:TPU:0, one launch (start us, length us, event | category | flops | bytes accessed | tf_op | source)
XLA Modules:
  0.0 351.5 jit_solution(16304407435643863073)
XLA Ops:
  9.9 1.1 fusion.132
  11.1 2.2 fusion.133
  13.3 1.3 collective-permute-start.1
  14.6 5.5 %collective-permute-start = (bf16[1,80,256]{2,1,0:T(8,128)(2,1)S(1)}, bf16[1,80,256]{2,1,0:T(8,128)(2,1)S(1)}, u32[]{:S(2)}, u32[]{:S(2)}) collective-permute-start(bf16[1,80,256]{2,1,0:T(8,128)(2,1)S(1)} %get-tuple-element.9), channel_id=1, source_target_pairs={{0,1},{1,2},{2,3},{3,4},{4,5},{5,6},{6,7},{8,9},{9,10},{10,11},{11... | collective-permute-start | bytes 122888 | tf_op jit(solution)/shard_map/ppermute | solution.py:27
  20.1 1.6 fusion.121
  26.7 1.2 fusion.135
  28.0 1.3 fusion.136
  29.3 1.3 collective-permute-start.3
  30.6 5.4 %collective-permute-start.2 = (bf16[1,80,256]{2,1,0:T(8,128)(2,1)S(1)}, bf16[1,80,256]{2,1,0:T(8,128)(2,1)S(1)}, u32[]{:S(2)}, u32[]{:S(2)}) collective-permute-start(bf16[1,80,256]{2,1,0:T(8,128)(2,1)S(1)} %get-tuple-element.7), channel_id=1, source_target_pairs={{0,1},{1,2},{2,3},{3,4},{4,5},{5,6},{6,7},{8,9},{9,10},{10,11},{11... | collective-permute-start | bytes 122888 | tf_op jit(solution)/shard_map/ppermute | solution.py:27
  36.4 1.3 collective-permute-done.2
  41.5 1.2 convolution_add_fusion.1
  44.4 64.2 %reduce-scatter.2.cloned.1.call-done = bf16[64,128]{1,0:T(8,128)(2,1)} async-done(((bf16[512,128]{1,0:T(8,128)(2,1)}), bf16[64,128]{1,0:T(8,128)(2,1)}) %reduce-scatter.2.cloned.1.call-update) | async-done | bytes 16400 | tf_op jit(solution)/shard_map/reduce_scatter | solution.py:207
  108.5 1.0 fusion.138
  109.8 2.8 fusion.31
  113.8 43.3 %all_gather.18 = bf16[512,1,16,48]{3,2,1,0:T(8,128)(2,1)S(1)} all-gather(bf16[64,1,16,48]{3,2,1,0:T(8,128)(2,1)S(1)} %bitcast.233), channel_id=1, replica_groups=mesh['sample'=4,'tok'=8] {'tok'}, dimensions={0}, use_global_device_ids=true | all-gather | bytes 884736 | tf_op jit(solution)/shard_map/all_gather | solution.py:155
  157.1 1.7 copy.66
  158.7 1.2 squeeze.47
  159.9 42.3 %all_gather.20 = bf16[512,1,16,48]{3,2,1,0:T(8,128)(2,1)S(1)} all-gather(bf16[64,1,16,48]{3,2,1,0:T(8,128)(2,1)S(1)} %bitcast.234), channel_id=1, replica_groups=mesh['sample'=4,'tok'=8] {'tok'}, dimensions={0}, use_global_device_ids=true | all-gather | bytes 884736 | tf_op jit(solution)/shard_map/all_gather | solution.py:156
  202.3 2.4 copy.69
  204.7 1.8 fusion.139
  207.4 2.4 fusion.140
  210.0 2.8 fusion.28
  213.3 41.5 %all_gather.21 = bf16[512,1,16,48]{3,2,1,0:T(8,128)(2,1)S(1)} all-gather(bf16[64,1,16,48]{3,2,1,0:T(8,128)(2,1)S(1)} %bitcast.235), channel_id=1, replica_groups=mesh['sample'=4,'tok'=8] {'tok'}, dimensions={0}, use_global_device_ids=true | all-gather | bytes 884736 | tf_op jit(solution)/shard_map/all_gather | solution.py:155
  254.8 1.7 copy.71
  256.5 1.8 fusion.145
  258.6 43.2 %all_gather.22 = bf16[512,1,16,48]{3,2,1,0:T(8,128)(2,1)} all-gather(bf16[64,1,16,48]{3,2,1,0:T(8,128)(2,1)S(1)} %bitcast.236), channel_id=1, replica_groups=mesh['sample'=4,'tok'=8] {'tok'}, dimensions={0}, use_global_device_ids=true | all-gather | bytes 884736 | tf_op jit(solution)/shard_map/all_gather | solution.py:156
  301.8 2.5 copy.74
  305.1 3.3 fusion.146
  309.1 1.1 multiply_reduce_fusion.3
  310.3 1.3 convolution_convert_fusion.1
  311.5 30.5 %all_gather.23 = bf16[512,128]{1,0:T(8,128)(2,1)S(1)} all-gather(bf16[64,128]{1,0:T(8,128)(2,1)S(1)} %convolution_convert_fusion.1), channel_id=1, replica_groups=mesh['sample'=4,'tok'=8] {'tok'}, dimensions={0}, use_global_device_ids=true | all-gather | bytes 147456 | tf_op jit(solution)/shard_map/all_gather | solution.py:234
  342.1 1.1 fusion.151
  (110 shorter events, 17.8 us)
Async XLA Ops:
  7.4 101.2 %copy-start = (bf16[128,768]{1,0:T(8,128)(2,1)S(1)}, bf16[128,768]{1,0:T(8,128)(2,1)}, u32[]{:S(2)}) copy-start(bf16[128,768]{1,0:T(8,128)(2,1)} %param.27) | copy-start | bytes 589828
  7.4 101.2 %reduce-scatter.2.cloned.1.call-start = ((), (), s32[]{:S(2)}) async-start(), calls=%async_computation.1 | async-start | bytes 147456 | tf_op jit(solution)/shard_map/reduce_scatter | solution.py:207
  13.3 8.8 %collective-permute-start.1 = (bf16[1,80,256]{2,1,0:T(8,128)(2,1)S(1)}, bf16[1,80,256]{2,1,0:T(8,128)(2,1)S(1)}, u32[]{:S(2)}, u32[]{:S(2)}) collective-permute-start(bf16[1,80,256]{2,1,0:T(8,128)(2,1)S(1)} %get-tuple-element.10), channel_id=1, source_target_pairs={{1,0},{2,1},{3,2},{4,3},{5,4},{6,5},{7,6},{9,8},{10,9},{11,10},{12... | collective-permute-start | bytes 122888 | tf_op jit(solution)/shard_map/ppermute | solution.py:30
  14.6 7.5 %collective-permute-start = (bf16[1,80,256]{2,1,0:T(8,128)(2,1)S(1)}, bf16[1,80,256]{2,1,0:T(8,128)(2,1)S(1)}, u32[]{:S(2)}, u32[]{:S(2)}) collective-permute-start(bf16[1,80,256]{2,1,0:T(8,128)(2,1)S(1)} %get-tuple-element.9), channel_id=1, source_target_pairs={{0,1},{1,2},{2,3},{3,4},{4,5},{5,6},{6,7},{8,9},{9,10},{10,11},{11... | collective-permute-start | bytes 122888 | tf_op jit(solution)/shard_map/ppermute | solution.py:27
  23.8 1.2 copy-start.3
  25.8 0.9 copy-start.12
  25.8 2.2 copy-start.6
  29.3 7.1 %collective-permute-start.3 = (bf16[1,80,256]{2,1,0:T(8,128)(2,1)S(1)}, bf16[1,80,256]{2,1,0:T(8,128)(2,1)S(1)}, u32[]{:S(2)}, u32[]{:S(2)}) collective-permute-start(bf16[1,80,256]{2,1,0:T(8,128)(2,1)S(1)} %get-tuple-element.8), channel_id=1, source_target_pairs={{1,0},{2,1},{3,2},{4,3},{5,4},{6,5},{7,6},{9,8},{10,9},{11,10},{12... | collective-permute-start | bytes 122888 | tf_op jit(solution)/shard_map/ppermute | solution.py:30
  30.6 7.1 %collective-permute-start.2 = (bf16[1,80,256]{2,1,0:T(8,128)(2,1)S(1)}, bf16[1,80,256]{2,1,0:T(8,128)(2,1)S(1)}, u32[]{:S(2)}, u32[]{:S(2)}) collective-permute-start(bf16[1,80,256]{2,1,0:T(8,128)(2,1)S(1)} %get-tuple-element.7), channel_id=1, source_target_pairs={{0,1},{1,2},{2,3},{3,4},{4,5},{5,6},{6,7},{8,9},{9,10},{10,11},{11... | collective-permute-start | bytes 122888 | tf_op jit(solution)/shard_map/ppermute | solution.py:27
  40.5 2.1 copy-start.11
  41.0 3.3 copy-start.14
  41.0 67.6 %copy-start.9 = (bf16[64,768]{1,0:T(8,128)(2,1)S(1)}, bf16[64,768]{1,0:T(8,128)(2,1)}, u32[]{:S(2)}) copy-start(bf16[64,768]{1,0:T(8,128)(2,1)} %param.22) | copy-start | bytes 294916
  42.7 69.9 %copy-start.4 = (f32[512,128]{0,1:T(8,128)}, f32[512,128]{0,1:T(8,128)S(1)}, u32[]{:S(2)}) copy-start(f32[512,128]{0,1:T(8,128)S(1)} %convolution_add_fusion.1) | copy-start | bytes 786436
  43.7 161.0 %all-gather.2.cloned.1.call-start = ((), (), s32[]{:S(2)}) async-start(), calls=%async_computation.2 | async-start | bytes 2621440 | tf_op jit(solution)/shard_map/all_gather | solution.py:220
  109.6 3.0 copy-start.1
  206.5 0.9 copy-start.2
  209.7 3.0 copy-start.7
  301.8 3.3 copy-start.8
  305.1 37.0 %copy-start.5 = (f32[512,128]{0,1:T(8,128)S(1)}, f32[512,128]{0,1:T(8,128)}, u32[]{:S(2)}) copy-start(f32[512,128]{0,1:T(8,128)} %copy-done.4) | copy-start | bytes 786436
  308.5 34.8 %copy-start.10 = (f32[1,3,512]{2,0,1:T(1,128)S(1)}, f32[1,3,512]{2,0,1:T(1,128)}, u32[]{:S(2)}) copy-start(f32[1,3,512]{2,0,1:T(1,128)} %param.16) | copy-start | bytes 18436
  308.5 34.8 %copy-start.13 = (bf16[3,128]{1,0:T(4,128)(2,1)S(1)}, bf16[3,128]{1,0:T(4,128)(2,1)}, u32[]{:S(2)}) copy-start(bf16[3,128]{1,0:T(4,128)(2,1)} %param.31) | copy-start | bytes 2308
Sparse Core Ops, SparseCore 0:
  43.8 64.6 reduce-scatter.1
Sparse Core Ops, SparseCore 1:
  45.7 26.3 all-gather.1
where the time goes:
time: 352 us; the launch traced here: 351 us
  blocking collectives  201 us (57%)
  waiting for transfers between devices  66 us (19%)
  matrix products  29 us (8%)
  local copies, waits for them, and re-layouts  19.5 us (6%)
  between operations  16.4 us (5%)
  starting transfers between devices  13.5 us (4%)
  other arithmetic  6.3 us (2%)
    all_gather x2, blocking collectives, sample_block(): lax.all_gather(value_rows, 'tok', axis=0, tiled=True)  85.5 us
    all_gather x2, blocking collectives, sample_block(): lax.all_gather(key_rows, 'tok', axis=0, tiled=True)  84.9 us
    reduce_scatter x1, waiting for transfers between devices, on_device(): lax.psum_scatter(jnp.dot(onehot, atom_rows, preferred_element_type=jnp.fl...  64.2 us
    all_gather x1, blocking collectives, on_device(): lax.all_gather(emit_rows, 'tok', axis=0, tiled=True)  30.5 us
    ppermute x2, starting transfers between devices, padded_2(): lax.ppermute(lax.slice_in_dim(block, block.shape[dim] - width, None, axis...  10.9 us
  transfers between devices with their start and end apart: 6, of which 2 were waited for; matrix products, arithmetic and copies ran while one was open for 4% of the time, Pallas kernels for 0%

commit v1 on v0

v1 whole, which is shorter than its diff:
```python
import functools
import math

import jax
import jax.numpy as jnp
from jax import lax
from jax.experimental import pallas as pl
from jax.experimental.pallas import tpu as pltpu
from jax.sharding import PartitionSpec as P

WQ = 32
WK = 128
HALO = (WK - WQ) // 2

MESH = pl.DeviceIdType.MESH
sigma_data = 16.0
sigma_peak = 160.0
sigma_floor = 0.0004
plan_steps = 200.0
norm_eps = 1e-05
masked_score = -1000000000.0
BF = jnp.bfloat16
F32 = jnp.float32
ANY = pl.BlockSpec(memory_space=pl.ANY)
VMEM = pl.BlockSpec(memory_space=pltpu.VMEM)


def noise_level(noise_step):
    fraction = noise_step[0].astype(jnp.float32) / plan_steps
    upper = sigma_peak ** (1.0 / 7.0)
    lower = sigma_floor ** (1.0 / 7.0)
    return sigma_data * (upper + fraction * (lower - upper)) ** 7


def layer_norm(values):
    centred = values - jnp.mean(values, axis=-1, keepdims=True)
    spread = jnp.mean(centred * centred, axis=-1, keepdims=True)
    return centred * lax.rsqrt(spread + norm_eps)


def dot(a, b):
    return jnp.dot(a, b, preferred_element_type=F32)


def dot_t(a, b):
    return lax.dot_general(a, b, (((1,), (1,)), ((), ())), preferred_element_type=F32)


def head_mask(head, head_dim, width, kind):
    lane = lax.broadcasted_iota(jnp.int32, (1, width), 1)
    inside = (lane >= head * head_dim) & (lane < (head + 1) * head_dim)
    return jnp.where(inside, 1.0, 0.0).astype(kind)


def step_kernel(
    n,
    s_count,
    act0,
    tok_row,
    tok_col,
    counts,
    atom_bias,
    token_single,
    pair_bias,
    w_atom,
    w_atom_out,
    w_tok_in,
    w_proj_hbm,
    w_out_hbm,
    w_tok_out,
    w_pos_out,
    update_ref,
    act,
    kv,
    gated,
    part,
    pool_in,
    mean_all,
    single_all,
    bias_all,
    normed_all,
    emit_all,
    w_proj,
    w_out,
    weight_sem,
    halo_send,
    halo_recv,
    bias_send,
    bias_recv,
    single_send,
    single_recv,
    pool_send,
    pool_recv,
    mean_send,
    mean_recv,
    norm_send,
    norm_recv,
    emit_send,
    emit_recv,
):
    me = lax.axis_index("tok")
    mine = lax.axis_index("sample")
    layers, width = w_atom.shape[0], w_atom.shape[1]
    atoms = act0.shape[0]
    heads = atom_bias.shape[1] // (layers * WK)
    head_dim = width // heads
    local = token_single.shape[0]
    tokens = n * local
    sent = []

    def push(src, dst, send, recv, where):
        copy = pltpu.make_async_remote_copy(
            src_ref=src, dst_ref=dst, send_sem=send, recv_sem=recv,
            device_id=where, device_id_type=MESH,
        )
        copy.start()
        sent.append(copy)
        return copy

    def peer(distance):
        return lax.rem(me + distance, n)

    def rows_of(index):
        return pl.ds(pl.multiple_of(index * local, local), local)

    def spread_rows(src, dst, send, recv):
        return [
            push(src, dst.at[rows_of(me)], send.at[d - 1], recv.at[d - 1], {"tok": peer(d)})
            for d in range(1, n)
        ]

    weights = [
        pltpu.make_async_copy(w_proj_hbm, w_proj, weight_sem.at[0]),
        pltpu.make_async_copy(w_out_hbm, w_out, weight_sem.at[1]),
    ]
    for copy in weights:
        copy.start()

    barrier = pltpu.get_barrier_semaphore()
    for d in range(1, n):
        pl.semaphore_signal(barrier, inc=1, device_id={"tok": peer(d)}, device_id_type=MESH)
    for d in range(1, s_count):
        pl.semaphore_signal(
            barrier, inc=1, device_id={"sample": lax.rem(mine + d, s_count)}, device_id_type=MESH
        )
    pl.semaphore_wait(barrier, n - 1 + s_count - 1)

    bias_copies = [
        push(
            pair_bias, bias_all.at[mine], bias_send.at[d - 1], bias_recv.at[d - 1],
            {"sample": lax.rem(mine + d, s_count)},
        )
        for d in range(1, s_count)
    ]
    bias_all[mine] = pair_bias[...]

    act[...] = act0[...]
    windows = atoms // WQ
    first = me * atoms
    atom_total = n * atoms
    lane = lax.broadcasted_iota(jnp.int32, (1, WK), 1)
    atom_masks = [head_mask(h, head_dim, width, BF) for h in range(heads)]
    atom_masks32 = [head_mask(h, head_dim, width, F32) for h in range(heads)]
    score_scale = 1.0 / math.sqrt(head_dim)
    single_copies = []
    for layer in range(layers):
        normed = layer_norm(act[...]).astype(BF)
        proj = dot(normed, w_atom[layer])
        kv[layer, HALO : HALO + atoms, :] = proj[:, width : 3 * width].astype(BF)
        here = kv.at[layer]
        halo = [
            push(
                here.at[pl.ds(HALO, HALO)], here.at[pl.ds(HALO + atoms, HALO)],
                halo_send.at[layer, 0], halo_recv.at[layer, 0], {"tok": peer(n - 1)},
            ),
            push(
                here.at[pl.ds(atoms, HALO)], here.at[pl.ds(0, HALO)],
                halo_send.at[layer, 1], halo_recv.at[layer, 1], {"tok": peer(1)},
            ),
        ]
        if layer == 0:
            single_copies = spread_rows(token_single, single_all, single_send, single_recv)
            single_all[rows_of(me), :] = token_single[...]
        queries = proj[:, :width].astype(BF)
        gates = jax.nn.sigmoid(proj[:, 3 * width :])
        inner = [w for w in range(windows) if WQ * w >= HALO and WQ * w + WK <= HALO + atoms]
        outer = [w for w in range(windows) if w not in inner]
        for w in inner + outer:
            if outer and w == outer[0]:
                for copy in halo:
                    copy.wait_recv()
            low = WQ * w
            keys = kv[layer, low : low + WK, :width]
            values = kv[layer, low : low + WK, width:]
            q = queries[low : low + WQ]
            stacked = jnp.concatenate([q * m for m in atom_masks], axis=0)
            bias = jnp.concatenate(
                [
                    atom_bias[low : low + WQ, (layer * heads + h) * WK : (layer * heads + h + 1) * WK]
                    for h in range(heads)
                ],
                axis=0,
            )
            scores = dot_t(stacked, keys) * score_scale + bias.astype(F32)
            if w in outer:
                position = first + (WQ * w - HALO) + lane
                valid = (position >= 0) & (position < atom_total)
                scores = jnp.where(valid, scores, masked_score)
            exponent = jnp.exp(scores - jnp.max(scores, axis=-1, keepdims=True))
            inverse = 1.0 / jnp.sum(exponent, axis=-1, keepdims=True)
            mixed = dot(exponent.astype(BF), values) * inverse
            total = mixed[:WQ] * atom_masks32[0]
            for h in range(1, heads):
                total = total + mixed[h * WQ : (h + 1) * WQ] * atom_masks32[h]
            gated[low : low + WQ, :] = (total * gates[low : low + WQ]).astype(BF)
        act[...] = act[...] + dot(gated[...], w_atom_out[layer])

    lifted = jnp.maximum(act[...], 0.0).astype(BF)
    owner = lax.broadcasted_iota(jnp.int32, (tokens, atoms), 0)
    onehot = jnp.where(owner == tok_row[...], 1.0, 0.0).astype(BF)
    part[...] = dot(onehot, lifted).astype(BF)
    pool_copies = [
        push(
            part.at[rows_of(peer(d))], pool_in.at[d - 1], pool_send.at[d - 1],
            pool_recv.at[d - 1], {"tok": peer(d)},
        )
        for d in range(1, n)
    ]
    pooled = part[rows_of(me), :].astype(F32)
    for d in range(1, n):
        pool_copies[d - 1].wait_recv()
        pooled = pooled + pool_in[d - 1].astype(F32)
    mean_all[rows_of(me), :] = (pooled / counts[...]).astype(BF)
    mean_copies = spread_rows(mean_all.at[rows_of(me)], mean_all, mean_send, mean_recv)

    model = token_single.shape[1]
    token_head_dim = w_out.shape[1] // (s_count * pair_bias.shape[1])
    span = 3 * 128
    per_group = span // token_head_dim
    per_source = pair_bias.shape[1]
    token_scale = 1.0 / math.sqrt(token_head_dim)
    token_masks = [head_mask(h, token_head_dim, span, BF) for h in range(per_group)]
    token_masks32 = [head_mask(h, token_head_dim, span, F32) for h in range(per_group)]

    def token_block(block, everyone, ours):
        q = dot(ours, w_proj[block, 0]).astype(BF)
        k = dot(everyone, w_proj[block, 1]).astype(BF)
        v = dot(everyone, w_proj[block, 2]).astype(BF)
        delta = None
        for group in range(model // span):
            cut = slice(group * span, (group + 1) * span)
            qg, kg, vg = q[:, cut], k[:, cut], v[:, cut]
            total = None
            for source in range(group * per_group // per_source, (group + 1) * per_group // per_source):
                start = source * per_source - group * per_group
                stacked = jnp.concatenate(
                    [qg * token_masks[start + h] for h in range(per_source)], axis=0
                )
                bias = jnp.concatenate(
                    [bias_all[source, block, h] for h in range(per_source)], axis=0
                )
                scores = dot_t(stacked, kg) * token_scale + bias.astype(F32)
                exponent = jnp.exp(scores - jnp.max(scores, axis=-1, keepdims=True))
                inverse = 1.0 / jnp.sum(exponent, axis=-1, keepdims=True)
                mixed = dot(exponent.astype(BF), vg) * inverse
                for h in range(per_source):
                    term = mixed[h * local : (h + 1) * local] * token_masks32[start + h]
                    total = term if total is None else total + term
            term = dot(total.astype(BF), w_out[block, cut, :])
            delta = term if delta is None else delta + term
        return delta

    for copy in single_copies:
        copy.wait_recv()
    for copy in weights:
        copy.wait()
    for copy in mean_copies:
        copy.wait_recv()
    token_all = single_all[...].astype(F32) + dot(mean_all[...], w_tok_in[...])
    normed_all[0] = layer_norm(token_all).astype(BF)
    token_act = token_single[...].astype(F32) + dot(mean_all[rows_of(me), :], w_tok_in[...])
    for copy in bias_copies:
        copy.wait_recv()
    blocks = w_proj.shape[0]
    for block in range(blocks):
        ours = normed_all[block, rows_of(me), :]
        token_act = token_act + token_block(block, normed_all[block], ours)
        if block + 1 < blocks:
            normed_all[block + 1, rows_of(me), :] = layer_norm(token_act).astype(BF)
            landing = normed_all.at[block + 1]
            for copy in spread_rows(
                landing.at[rows_of(me)], landing, norm_send.at[block], norm_recv.at[block]
            ):
                copy.wait_recv()

    emit_all[rows_of(me), :] = dot(layer_norm(token_act).astype(BF), w_tok_out[...]).astype(BF)
    emit_copies = spread_rows(emit_all.at[rows_of(me)], emit_all, emit_send, emit_recv)
    owner = lax.broadcasted_iota(jnp.int32, (atoms, tokens), 1)
    onehot = jnp.where(owner == tok_col[...], 1.0, 0.0).astype(BF)
    for copy in emit_copies:
        copy.wait_recv()
    final = act[...] + dot(onehot, emit_all[...])
    update_ref[...] = dot_t(w_pos_out[...], layer_norm(final).astype(BF))
    for copy in sent:
        copy.wait_send()


def on_device(
    n,
    s_count,
    noisy_pos,
    noise_step,
    atom_single,
    atom_token,
    token_counts,
    atom_bias,
    token_single,
    pair_bias,
    w_pos,
    w_atom,
    w_atom_out,
    w_tok_in,
    w_proj,
    w_out,
    w_tok_out,
    w_pos_out,
):
    position = noisy_pos[0]
    atoms = position.shape[1]
    local, model = token_single.shape
    width = atom_single.shape[1]
    tokens = local * n
    layers = w_atom.shape[0]
    blocks = w_proj.shape[0]
    sigma = noise_level(noise_step)
    square = sigma * sigma + sigma_data * sigma_data
    scale_in = 1.0 / jnp.sqrt(square)
    scale_skip = sigma_data * sigma_data / square
    scale_out = sigma * sigma_data / jnp.sqrt(square)
    act0 = atom_single.astype(F32) + jnp.dot(
        jnp.transpose(position * scale_in), w_pos, precision=lax.Precision.HIGHEST
    )
    dma = pltpu.SemaphoreType.DMA
    update = pl.pallas_call(
        functools.partial(step_kernel, n, s_count),
        out_shape=jax.ShapeDtypeStruct((16, atoms), F32),
        in_specs=[VMEM] * 10 + [ANY] * 2 + [VMEM] * 2,
        out_specs=VMEM,
        scratch_shapes=[
            pltpu.VMEM((atoms, width), F32),
            pltpu.VMEM((layers, atoms + 2 * HALO, 2 * width), BF),
            pltpu.VMEM((atoms, width), BF),
            pltpu.VMEM((tokens, width), BF),
            pltpu.VMEM((n - 1, local, width), BF),
            pltpu.VMEM((tokens, width), BF),
            pltpu.VMEM((tokens, model), BF),
            pltpu.VMEM((s_count,) + pair_bias.shape, BF),
            pltpu.VMEM((blocks, tokens, model), BF),
            pltpu.VMEM((tokens, width), BF),
            pltpu.VMEM(w_proj.shape, BF),
            pltpu.VMEM((blocks, model, model), BF),
            dma((2,)),
            dma((layers, 2)),
            dma((layers, 2)),
            dma((s_count - 1,)),
            dma((s_count - 1,)),
            dma((n - 1,)),
            dma((n - 1,)),
            dma((n - 1,)),
            dma((n - 1,)),
            dma((n - 1,)),
            dma((n - 1,)),
            dma((blocks - 1, n - 1)),
            dma((blocks - 1, n - 1)),
            dma((n - 1,)),
            dma((n - 1,)),
        ],
        compiler_params=pltpu.CompilerParams(
            collective_id=0, has_side_effects=True, vmem_limit_bytes=58 * 2**20
        ),
    )(
        act0,
        atom_token.reshape(1, atoms),
        atom_token.reshape(atoms, 1),
        token_counts.astype(F32).reshape(local, 1),
        atom_bias.reshape(atoms, -1),
        token_single,
        pair_bias,
        w_atom,
        w_atom_out,
        w_tok_in,
        w_proj,
        w_out.reshape(blocks, model, model),
        w_tok_out,
        jnp.pad(w_pos_out, ((0, 16 - w_pos_out.shape[0]), (0, 0))),
    )[: position.shape[0]]
    return ((scale_skip * position + scale_out * update) / sigma_data)[None]


def solution(mesh):
    in_specs = (
        P("sample", None, "tok"),
        P(),
        P("tok", None),
        P("tok"),
        P("tok"),
        P("tok", None, None, None),
        P("tok", None),
        P(None, "sample", "tok", None),
        P(),
        P(),
        P(),
        P(),
        P(),
        P(),
        P(),
        P(),
    )
    return jax.shard_map(
        functools.partial(on_device, mesh.shape["tok"], mesh.shape["sample"]),
        mesh=mesh,
        in_specs=in_specs,
        out_specs=P("sample", None, "tok"),
        check_vma=False,
    )
```

time: 352 us -> 83.1 us (0.24)
  blocking collectives: 201 us -> 0 us
  Pallas kernels: 0 us -> 70.9 us
  waiting for transfers between devices: 66 us -> 0 us
  matrix products: 29 us -> 2.22 us
  between operations: 16.4 us -> 0.86 us
  starting transfers between devices: 13.5 us -> 0 us
  local copies, waits for them, and re-layouts: 19.5 us -> 6.7 us
  other arithmetic: 6.3 us -> 2.08 us
    all_gather x5 -> x0, blocking collectives: 201 us -> none  [the longest x2 85.5 us: sample_block(): lax.all_gather(value_rows, 'tok', axis=0, tiled=True)]
    pallas_call x0 -> x1, Pallas kernels: none -> 70.9 us  [on_device(): pl.pallas_call(functools.partial(step_kernel, n, s_count), out_shape=jax....]
    reduce_scatter x1 -> x0, waiting for transfers between devices: 64.2 us -> none  [on_device(): lax.psum_scatter(jnp.dot(onehot, atom_rows, preferred_element_type=jnp.fl...]
    dot_general x20 -> x1, matrix products: 29 us -> 2.22 us  [on_device(): jnp.dot(jnp.transpose(position * scale_in), w_pos, precision=lax.Precisio...]
    ppermute x4 -> x0, starting transfers between devices: 13.5 us -> none  [the longest x2 10.9 us: padded_2(): lax.ppermute(lax.slice_in_dim(block, block.shape[dim] - width, None, axis...]
    all_gather x4 -> x0, local copies, waits for them, and re-layouts: 8.25 us -> none  [the longest x2 4.94 us: sample_block(): lax.all_gather(value_rows, 'tok', axis=0, tiled=True)]
    reduce_sum x10 -> x0, other arithmetic: 4.51 us -> none  [the longest x6 1.63 us: layer_norm(): spread = jnp.mean(centred * centred, axis=-1, keepdims=True)]
    reshape x2 -> x3, local copies, waits for them, and re-layouts: 0.93 us -> 4.82 us  [the longest x1 2.58 us: on_device(): atom_bias.reshape(atoms, -1)]
  transfers between devices with their start and end apart: 6 -> 0, of which waited for: 2 -> 0; matrix products, arithmetic and copies ran while one was open for 4% -> 0% of each run, Pallas kernels for 0% -> 0%
where the time goes in v1:
time: 83.1 us; the launch traced here: 82.8 us
  Pallas kernels  70.9 us (85%)
  local copies, waits for them, and re-layouts  6.7 us (8%)
  matrix products  2.22 us (3%)
  other arithmetic  2.08 us (3%)
  between operations  0.86 us (1%)
    pallas_call x1, Pallas kernels, on_device(): pl.pallas_call(functools.partial(step_kernel, n, s_count), out_shape=jax....  70.9 us
    reshape x1, local copies, waits for them, and re-layouts, on_device(): atom_bias.reshape(atoms, -1)  2.58 us
    dot_general x1, matrix products, on_device(): jnp.dot(jnp.transpose(position * scale_in), w_pos, precision=lax.Precisio...  2.22 us

profile of v1, /device:TPU:0, one launch (start us, length us, event | category | flops | bytes accessed | tf_op | source)
XLA Modules:
  0.0 82.8 jit_solution(8454934333059218930)
XLA Ops:
  0.0 0.0 copy-start
  0.8 0.7 convert_bitcast_fusion
  1.5 1.3 %pad.4.w_pos_out = bf16[16,128]{1,0:T(8,128)(2,1)} pad(bf16[3,128]{1,0:T(4,128)(2,1)} %param.31, bf16[]{:T(256)} %constant.20.clone.1), padding=0_13x0_0 | pad | bytes 4866 | tf_op jit(solution)/shard_map/jit(_pad)/pad | solution.py:395
  2.8 0.7 broadcast_multiply_fusion
  3.5 0.7 copy.22.counts
  4.2 0.0 copy-done
  4.2 2.2 %convolution_add_fusion.act0 = f32[512,128]{1,0:T(8,128)} fusion(f32[3,128]{1,0:T(4,128)S(1)} %copy-done, bf16[512,128]{1,0:T(8,128)(2,1)} %param.18, f32[1,3,512]{2,0,1:T(1,128)S(1)} %broadcast_multiply_fusion), kind=kOutput, calls=%fused_computation | convolution fusion | flops 2490368 | bytes 400896 | tf_op jit(solution)/shard_map/dot_general | solution.py:340
  6.4 1.5 %copy.21.tok_col = s32[512,1]{1,0:T(8,128)} copy(s32[512,1]{0,1:T(1,128)} %bitcast.19) | data formatting | bytes 4096 | tf_op jit(solution)/shard_map/reshape | solution.py:384
  7.9 0.0 copy-start.1
  7.9 2.6 %reshape.27.atom_bias = bf16[512,1024]{1,0:T(8,128)(2,1)} reshape(bf16[512,2,4,128]{3,2,1,0:T(4,128)(2,1)} %param.21) | data formatting | bytes 2097152 | tf_op jit(solution)/shard_map/reshape | solution.py:386
  10.5 70.9 %shard_map.154 = f32[16,512]{1,0:T(8,128)} custom-call(f32[512,128]{1,0:T(8,128)} %convolution_add_fusion.act0, s32[1,512]{1,0:T(1,128)} %bitcast.20, s32[512,1]{1,0:T(8,128)} %copy.21.tok_col, f32[64,1]{1,0:T(8,128)} %copy.22.counts, bf16[512,1024]{1,0:T(8,128)(2,1)} %reshape.27.atom_bias, bf16[64,768]{1,0:T(8,128)(2,1)} %token_single.1, ...), custom_call_target="tpu_custom_call" | custom-call | tf_op jit(solution)/shard_map/pallas_call | solution.py:344
  81.4 0.0 copy-done.1
  81.5 0.7 fusion.3
  82.2 0.6 copy.23
Async XLA Ops:
  0.0 4.2 %copy-start = (f32[3,128]{1,0:T(4,128)S(1)}, f32[3,128]{1,0:T(4,128)}, u32[]{:S(2)}) copy-start(f32[3,128]{1,0:T(4,128)} %param.24) | copy-start | bytes 4612
  7.9 73.5 %copy-start.1 = (f32[1,3,512]{2,0,1:T(1,128)S(1)}, f32[1,3,512]{2,0,1:T(1,128)}, u32[]{:S(2)}) copy-start(f32[1,3,512]{2,0,1:T(1,128)} %param.16) | copy-start | bytes 18436

commit v2 on v1

--- a/solution.py
+++ b/solution.py
@@ -26,7 +26,7 @@
 
 
 def noise_level(noise_step):
-    fraction = noise_step[0].astype(jnp.float32) / plan_steps
+    fraction = noise_step.astype(jnp.float32) / plan_steps
     upper = sigma_peak ** (1.0 / 7.0)
     lower = sigma_floor ** (1.0 / 7.0)
     return sigma_data * (upper + fraction * (lower - upper)) ** 7
@@ -55,13 +55,15 @@
 def step_kernel(
     n,
     s_count,
-    act0,
+    noise_step,
+    noisy_pos,
+    atom_single,
     tok_row,
-    tok_col,
     counts,
     atom_bias,
     token_single,
     pair_bias,
+    w_pos,
     w_atom,
     w_atom_out,
     w_tok_in,
@@ -69,7 +71,7 @@
     w_out_hbm,
     w_tok_out,
     w_pos_out,
-    update_ref,
+    out_ref,
     act,
     kv,
     gated,
@@ -89,6 +91,8 @@
     bias_recv,
     single_send,
     single_recv,
+    relay_send,
+    relay_recv,
     pool_send,
     pool_recv,
     mean_send,
@@ -101,8 +105,8 @@
     me = lax.axis_index("tok")
     mine = lax.axis_index("sample")
     layers, width = w_atom.shape[0], w_atom.shape[1]
-    atoms = act0.shape[0]
-    heads = atom_bias.shape[1] // (layers * WK)
+    atoms = atom_single.shape[0]
+    heads = atom_bias.shape[0] // (atoms * layers)
     head_dim = width // heads
     local = token_single.shape[0]
     tokens = n * local
@@ -129,6 +133,22 @@
             for d in range(1, n)
         ]
 
+    def relay_rows(landing, send, recv):
+        partner = me + 1 - 2 * lax.rem(me, 2)
+        half = n // 2
+
+        def hand(index, slot, target):
+            block = landing.at[rows_of(index)]
+            return push(block, block, send.at[slot], recv.at[slot], {"tok": target})
+
+        beside = [hand(me, 0, partner)]
+        along = [hand(me, i, peer(2 * i)) for i in range(1, half)]
+        for i in range(1, half):
+            along[i - 1].wait_recv()
+            beside.append(hand(peer(n - 2 * i), half - 1 + i, partner))
+        for copy in beside:
+            copy.wait_recv()
+
     weights = [
         pltpu.make_async_copy(w_proj_hbm, w_proj, weight_sem.at[0]),
         pltpu.make_async_copy(w_out_hbm, w_out, weight_sem.at[1]),
@@ -145,16 +165,32 @@
         )
     pl.semaphore_wait(barrier, n - 1 + s_count - 1)
 
-    bias_copies = [
-        push(
-            pair_bias, bias_all.at[mine], bias_send.at[d - 1], bias_recv.at[d - 1],
-            {"sample": lax.rem(mine + d, s_count)},
-        )
-        for d in range(1, s_count)
-    ]
+    def send_bias(block):
+        return [
+            push(
+                pair_bias.at[block], bias_all.at[mine, block], bias_send.at[block, d - 1],
+                bias_recv.at[block, d - 1], {"sample": lax.rem(mine + d, s_count)},
+            )
+            for d in range(1, s_count)
+        ]
+
+    bias_copies = [send_bias(0)]
     bias_all[mine] = pair_bias[...]
 
-    act[...] = act0[...]
+    shares, share_rows = single_all.shape[1], single_all.shape[2]
+    share = lax.rem(mine, shares)
+    share_at = pl.ds(pl.multiple_of(share * share_rows, share_rows), share_rows)
+
+    sigma = noise_level(jnp.full((1, 1), noise_step[0], jnp.int32))
+    square = sigma * sigma + sigma_data * sigma_data
+    position = noisy_pos[0]
+    act[...] = atom_single[...].astype(F32) + lax.dot_general(
+        position * (1.0 / jnp.sqrt(square)), w_pos[...], (((0,), (0,)), ((), ())),
+        precision=lax.Precision.HIGHEST, preferred_element_type=F32,
+    )
+    stacked_row = lax.broadcasted_iota(jnp.int32, (heads * WQ, WQ * layers * heads), 0)
+    bias_row = lax.broadcasted_iota(jnp.int32, (heads * WQ, WQ * layers * heads), 1)
+    wanted = (stacked_row & (WQ - 1)) * (layers * heads) + lax.shift_right_logical(stacked_row, 5)
     windows = atoms // WQ
     first = me * atoms
     atom_total = n * atoms
@@ -179,8 +215,15 @@
             ),
         ]
         if layer == 0:
-            single_copies = spread_rows(token_single, single_all, single_send, single_recv)
-            single_all[rows_of(me), :] = token_single[...]
+            single_copies = [
+                push(
+                    token_single.at[share_at], single_all.at[me, share],
+                    single_send.at[d - 1], single_recv.at[d - 1], {"tok": peer(d)},
+                )
+                for d in range(1, n)
+            ]
+            single_all[me, share] = token_single[share_at, :]
+        chooser = jnp.where(bias_row == wanted + layer * heads, 1.0, 0.0).astype(BF)
         queries = proj[:, :width].astype(BF)
         gates = jax.nn.sigmoid(proj[:, 3 * width :])
         inner = [w for w in range(windows) if WQ * w >= HALO and WQ * w + WK <= HALO + atoms]
@@ -194,17 +237,12 @@
             values = kv[layer, low : low + WK, width:]
             q = queries[low : low + WQ]
             stacked = jnp.concatenate([q * m for m in atom_masks], axis=0)
-            bias = jnp.concatenate(
-                [
-                    atom_bias[low : low + WQ, (layer * heads + h) * WK : (layer * heads + h + 1) * WK]
-                    for h in range(heads)
-                ],
-                axis=0,
-            )
-            scores = dot_t(stacked, keys) * score_scale + bias.astype(F32)
+            tall = WQ * layers * heads
+            bias = dot(chooser, atom_bias[w * tall : (w + 1) * tall, :])
+            scores = dot_t(stacked, keys) * score_scale + bias
             if w in outer:
-                position = first + (WQ * w - HALO) + lane
-                valid = (position >= 0) & (position < atom_total)
+                place = first + (WQ * w - HALO) + lane
+                valid = (place >= 0) & (place < atom_total)
                 scores = jnp.where(valid, scores, masked_score)
             exponent = jnp.exp(scores - jnp.max(scores, axis=-1, keepdims=True))
             inverse = 1.0 / jnp.sum(exponent, axis=-1, keepdims=True)
@@ -214,6 +252,19 @@
                 total = total + mixed[h * WQ : (h + 1) * WQ] * atom_masks32[h]
             gated[low : low + WQ, :] = (total * gates[low : low + WQ]).astype(BF)
         act[...] = act[...] + dot(gated[...], w_atom_out[layer])
+        if layer == 0:
+            for copy in single_copies:
+                copy.wait_recv()
+            relay_copies = [
+                push(
+                    single_all.at[:, share], single_all.at[:, share],
+                    relay_send.at[d - 1], relay_recv.at[d - 1],
+                    {"sample": mine - share + lax.rem(share + d, shares)},
+                )
+                for d in range(1, shares)
+            ]
+            for block in range(1, pair_bias.shape[0]):
+                bias_copies.append(send_bias(block))
 
     lifted = jnp.maximum(act[...], 0.0).astype(BF)
     owner = lax.broadcasted_iota(jnp.int32, (tokens, atoms), 0)
@@ -230,7 +281,13 @@
     for d in range(1, n):
         pool_copies[d - 1].wait_recv()
         pooled = pooled + pool_in[d - 1].astype(F32)
-    mean_all[rows_of(me), :] = (pooled / counts[...]).astype(BF)
+    diagonal = lax.broadcasted_iota(jnp.int32, (local, local), 0) == lax.broadcasted_iota(
+        jnp.int32, (local, local), 1
+    )
+    divisor = jnp.sum(
+        jnp.where(diagonal, counts[...].astype(F32), 0.0), axis=1, keepdims=True
+    )
+    mean_all[rows_of(me), :] = (pooled / divisor).astype(BF)
     mean_copies = spread_rows(mean_all.at[rows_of(me)], mean_all, mean_send, mean_recv)
 
     model = token_single.shape[1]
@@ -270,37 +327,36 @@
             delta = term if delta is None else delta + term
         return delta
 
-    for copy in single_copies:
+    for copy in relay_copies:
         copy.wait_recv()
     for copy in weights:
         copy.wait()
     for copy in mean_copies:
         copy.wait_recv()
-    token_all = single_all[...].astype(F32) + dot(mean_all[...], w_tok_in[...])
+    token_all = single_all[...].reshape(tokens, model).astype(F32) + dot(mean_all[...], w_tok_in[...])
     normed_all[0] = layer_norm(token_all).astype(BF)
     token_act = token_single[...].astype(F32) + dot(mean_all[rows_of(me), :], w_tok_in[...])
-    for copy in bias_copies:
-        copy.wait_recv()
     blocks = w_proj.shape[0]
     for block in range(blocks):
+        for copy in bias_copies[block]:
+            copy.wait_recv()
         ours = normed_all[block, rows_of(me), :]
         token_act = token_act + token_block(block, normed_all[block], ours)
         if block + 1 < blocks:
             normed_all[block + 1, rows_of(me), :] = layer_norm(token_act).astype(BF)
-            landing = normed_all.at[block + 1]
-            for copy in spread_rows(
-                landing.at[rows_of(me)], landing, norm_send.at[block], norm_recv.at[block]
-            ):
-                copy.wait_recv()
+            relay_rows(normed_all.at[block + 1], norm_send.at[block], norm_recv.at[block])
 
     emit_all[rows_of(me), :] = dot(layer_norm(token_act).astype(BF), w_tok_out[...]).astype(BF)
     emit_copies = spread_rows(emit_all.at[rows_of(me)], emit_all, emit_send, emit_recv)
-    owner = lax.broadcasted_iota(jnp.int32, (atoms, tokens), 1)
-    onehot = jnp.where(owner == tok_col[...], 1.0, 0.0).astype(BF)
     for copy in emit_copies:
         copy.wait_recv()
-    final = act[...] + dot(onehot, emit_all[...])
-    update_ref[...] = dot_t(w_pos_out[...], layer_norm(final).astype(BF))
+    final = act[...] + lax.dot_general(
+        onehot, emit_all[...], (((0,), (0,)), ((), ())), preferred_element_type=F32
+    )
+    update = dot_t(w_pos_out[...], layer_norm(final).astype(BF))
+    scale_skip = sigma_data * sigma_data / square
+    scale_out = sigma * sigma_data / jnp.sqrt(square)
+    out_ref[0] = (scale_skip * position + scale_out * update) / sigma_data
     for copy in sent:
         copy.wait_send()
 
@@ -325,26 +381,18 @@
     w_tok_out,
     w_pos_out,
 ):
-    position = noisy_pos[0]
-    atoms = position.shape[1]
+    atoms = noisy_pos.shape[2]
     local, model = token_single.shape
     width = atom_single.shape[1]
     tokens = local * n
     layers = w_atom.shape[0]
     blocks = w_proj.shape[0]
-    sigma = noise_level(noise_step)
-    square = sigma * sigma + sigma_data * sigma_data
-    scale_in = 1.0 / jnp.sqrt(square)
-    scale_skip = sigma_data * sigma_data / square
-    scale_out = sigma * sigma_data / jnp.sqrt(square)
-    act0 = atom_single.astype(F32) + jnp.dot(
-        jnp.transpose(position * scale_in), w_pos, precision=lax.Precision.HIGHEST
-    )
+    shares = 4 if s_count % 4 == 0 else s_count
     dma = pltpu.SemaphoreType.DMA
-    update = pl.pallas_call(
+    return pl.pallas_call(
         functools.partial(step_kernel, n, s_count),
-        out_shape=jax.ShapeDtypeStruct((16, atoms), F32),
-        in_specs=[VMEM] * 10 + [ANY] * 2 + [VMEM] * 2,
+        out_shape=jax.ShapeDtypeStruct(noisy_pos.shape, F32),
+        in_specs=[pl.BlockSpec(memory_space=pltpu.SMEM)] + [VMEM] * 11 + [ANY] * 2 + [VMEM] * 2,
         out_specs=VMEM,
         scratch_shapes=[
             pltpu.VMEM((atoms, width), F32),
@@ -353,7 +401,7 @@
             pltpu.VMEM((tokens, width), BF),
             pltpu.VMEM((n - 1, local, width), BF),
             pltpu.VMEM((tokens, width), BF),
-            pltpu.VMEM((tokens, model), BF),
+            pltpu.VMEM((n, shares, local // shares, model), BF),
             pltpu.VMEM((s_count,) + pair_bias.shape, BF),
             pltpu.VMEM((blocks, tokens, model), BF),
             pltpu.VMEM((tokens, width), BF),
@@ -362,10 +410,12 @@
             dma((2,)),
             dma((layers, 2)),
             dma((layers, 2)),
-            dma((s_count - 1,)),
-            dma((s_count - 1,)),
-            dma((n - 1,)),
-            dma((n - 1,)),
+            dma((blocks, s_count - 1)),
+            dma((blocks, s_count - 1)),
+            dma((n - 1,)),
+            dma((n - 1,)),
+            dma((shares - 1,)),
+            dma((shares - 1,)),
             dma((n - 1,)),
             dma((n - 1,)),
             dma((n - 1,)),
@@ -379,22 +429,23 @@
             collective_id=0, has_side_effects=True, vmem_limit_bytes=58 * 2**20
         ),
     )(
-        act0,
+        noise_step,
+        noisy_pos,
+        atom_single,
         atom_token.reshape(1, atoms),
-        atom_token.reshape(atoms, 1),
-        token_counts.astype(F32).reshape(local, 1),
-        atom_bias.reshape(atoms, -1),
+        token_counts.reshape(1, local),
+        atom_bias.reshape(-1, WK),
         token_single,
         pair_bias,
+        w_pos,
         w_atom,
         w_atom_out,
         w_tok_in,
         w_proj,
         w_out.reshape(blocks, model, model),
         w_tok_out,
-        jnp.pad(w_pos_out, ((0, 16 - w_pos_out.shape[0]), (0, 0))),
-    )[: position.shape[0]]
-    return ((scale_skip * position + scale_out * update) / sigma_data)[None]
+        w_pos_out,
+    )
 
 
 def solution(mesh):

time: 83.1 us -> 64.5 us (0.78)
  Pallas kernels: 70.9 us -> 61.1 us
  local copies, waits for them, and re-layouts: 6.7 us -> 2.59 us
  matrix products: 2.22 us -> 0 us
  other arithmetic: 2.08 us -> 0 us
    pallas_call x1, Pallas kernels: 70.9 us -> 61.1 us  [on_device(): pl.pallas_call(functools.partial(step_kernel, n, s_count), out_shape=jax....]
    reshape x3 -> x0, local copies, waits for them, and re-layouts: 4.82 us -> none  [the longest x1 2.58 us: on_device(): atom_bias.reshape(atoms, -1)]
    dot_general x1 -> x0, matrix products: 2.22 us -> none  [on_device(): jnp.dot(jnp.transpose(position * scale_in), w_pos, precision=lax.Precisio...]
    pallas_call x0 -> x1, local copies, waits for them, and re-layouts: none -> 1.3 us  [on_device(): pl.pallas_call(functools.partial(step_kernel, n, s_count), out_shape=jax....]
    unnamed x4 -> x1, local copies, waits for them, and re-layouts: 0.01 us -> 1.29 us
    pad x1 -> x0, local copies, waits for them, and re-layouts: 1.28 us -> none  [on_device(): jnp.pad(w_pos_out, ((0, 16 - w_pos_out.shape[0]), (0, 0)))]
where the time goes in v2:
time: 64.5 us; the launch traced here: 64.3 us
  Pallas kernels  61.1 us (95%)
  local copies, waits for them, and re-layouts  2.59 us (4%)
  between operations  0.66 us (1%)
    pallas_call x1, Pallas kernels, on_device(): pl.pallas_call(functools.partial(step_kernel, n, s_count), out_shape=jax....  61.1 us
    pallas_call x1, local copies, waits for them, and re-layouts, on_device(): pl.pallas_call(functools.partial(step_kernel, n, s_count), out_shape=jax....  1.3 us

profile of v2, /device:TPU:0, one launch (start us, length us, event | category | flops | bytes accessed | tf_op | source)
XLA Modules:
  0.0 64.3 jit_solution(11315152380573185238)
XLA Ops:
  0.7 1.3 %copy.17.noisy_pos = f32[1,3,512]{2,1,0:T(4,128)} copy(f32[1,3,512]{2,0,1:T(1,128)} %param.16) | data formatting | bytes 12288 | tf_op args[0]
  1.9 61.1 %shard_map.154 = f32[1,3,512]{2,1,0:T(4,128)} custom-call(s32[1]{0:T(128)S(6)} %copy.19.noise_step, f32[1,3,512]{2,1,0:T(4,128)} %copy.17.noisy_pos, bf16[512,128]{1,0:T(8,128)(2,1)} %atom_single.1, s32[1,512]{1,0:T(1,128)} %bitcast.6, s32[1,64]{1,0:T(1,128)} %bitcast.7, bf16[4096,128]{1,0:T(8,128)(2,1)} %bitcast.5, bf16[64,768]{1,0:T(8,128)(2,1)} %token_single.1, ...), custom_call_target="tpu_custom_call" | custom-call | tf_op jit(solution)/shard_map/pallas_call | solution.py:392
  63.0 1.3 %copy.18 = f32[1,3,512]{2,0,1:T(1,128)} copy(f32[1,3,512]{2,1,0:T(4,128)} %shard_map.154) | data formatting | bytes 12288 | tf_op jit(solution)/shard_map/pallas_call | solution.py:392
